TPU v7x, 32 devices: a whole 2x2x4 slice. The times are simulated.
32 devices in a mesh: frames: 16 (over z, y, core), heads: 2 (over x).
Axes of the slice: x: 2, y: 2, z: 4, core: 2. Of those that a mesh axis runs over, the one named last changes fastest.
Arguments:
- frames_x: bfloat16 [16, 4, 80, 2240], P('frames', 'heads'), may hold values from -6 to 6
- qkv_weight: bfloat16 [3, 896, 4480], P(None, 'heads'), may hold values from -0.125 to 0.125
- out_weight: bfloat16 [1792, 2240], P('heads', 'frames'), may hold values from -0.125 to 0.125
Outputs:
- attn_out: bfloat16 [16, 4, 80, 2240], P('frames', 'heads')
All inputs are finite; a program needn't handle non-finite values.
Results may differ from a plain program's by a relative error of at most 0.005.
Values may be sent and summed in bfloat16 or wider, within the bound.
A program may use at most 128 MiB of HBM per device.

v0:
```python
import jax
import jax.numpy as jnp
from jax import lax
from jax.sharding import PartitionSpec as P

HD = 112


EPSILON = 1e-06


def carried_in(part, axis, combine, identity):
    place = lax.axis_index(axis)
    gathered = jax.tree.map(lambda a: lax.all_gather(a, axis), part)
    state = jax.tree.map(lambda a, e: jnp.zeros_like(a) + jnp.asarray(e, a.dtype), part, identity)

    def one(turn, state):
        return combine(
            state, jax.tree.map(lambda a: lax.dynamic_index_in_dim(a, turn, 0, False), gathered)
        )

    return lax.fori_loop(0, place, one, state)


def add_states(earlier, later):
    return (earlier[0] + later[0], earlier[1] + later[1])


def on_device(frames_x, qkv_weight, out_weight):
    feature_count = qkv_weight.shape[2] // 2
    local_width = qkv_weight.shape[1] * 2
    head_count = local_width // HD
    highest = lax.Precision.HIGHEST
    weights = qkv_weight.reshape(3, local_width, feature_count)
    mixed = jnp.einsum(
        "frcd,sed->sfrce",
        lax.all_gather(frames_x, "heads", axis=1, tiled=True),
        weights,
        preferred_element_type=jnp.float32,
    )
    projected = jnp.stack([jax.nn.relu(mixed[0]), jax.nn.relu(mixed[1]), mixed[2]]).astype(
        jnp.bfloat16
    )
    frame_count, row_count, col_count = (projected.shape[1], projected.shape[2], projected.shape[3])
    tokens = frame_count * row_count * col_count
    query = projected[0].reshape(tokens, head_count, HD)
    keys = projected[1].reshape(tokens, head_count, HD)
    values = projected[2].reshape(tokens, head_count, HD)
    own_state = jnp.einsum("mhi,mhj->hij", keys, values, preferred_element_type=jnp.float32)
    own_total = jnp.sum(keys.astype(jnp.float32), axis=0)
    identity = (jnp.zeros_like(own_state), jnp.zeros_like(own_total))
    prior_state, prior_total = carried_in((own_state, own_total), "frames", add_states, identity)
    query_wide = query.astype(jnp.float32)
    numerator = jnp.einsum("mhi,hij->mhj", query_wide, prior_state + own_state, precision=highest)
    denominator = (
        jnp.einsum("mhi,hi->mh", query_wide, prior_total + own_total, precision=highest) + EPSILON
    )
    attended = (numerator / denominator[..., None]).astype(jnp.bfloat16)
    attended = attended.reshape(frame_count, row_count, col_count, local_width)
    by_rows = lax.all_to_all(attended, "heads", split_axis=1, concat_axis=3, tiled=True)
    full_rows = lax.all_gather(out_weight, "heads", axis=0, tiled=True)
    result = jnp.einsum(
        "frce,ed->frcd",
        by_rows,
        lax.all_gather(full_rows, "frames", axis=1, tiled=True),
        preferred_element_type=jnp.float32,
    )
    return result.astype(jnp.bfloat16)


def solution(mesh):
    in_specs = (P("frames", "heads", None, None), P(None, "heads", None), P("heads", "frames"))
    out_specs = P("frames", "heads", None, None)
    return jax.shard_map(
        on_device, mesh=mesh, in_specs=in_specs, out_specs=out_specs, check_vma=False
    )
```

profile of v0, /device:TPU:0, one launch (start us, length us, event | category | flops | bytes accessed | tf_op | source)
XLA Modules:
  0.0 216.3 jit_solution(11924914860912711841)
XLA Ops:
  6.5 0.0 all-gather.6.cloned.1.call-start
  6.5 0.7 all-gather.6.cloned.1.call-update
  7.3 0.0 all-gather.8.cloned.1.call-start
  7.3 19.5 %reshape.65 = bf16[3,896,2240]{2,1,0:T(8,128)(2,1)} reshape(bf16[3,448,4480]{2,1,0:T(8,128)(2,1)} %param.6) | data formatting | bytes 24084480 | tf_op jit(solution)/shard_map/reshape | solution.py:34
  26.8 10.9 %all-gather.6.cloned.1.call-done = bf16[1,4,80,2240]{3,2,0,1:T(8,128)(2,1)} async-done(((bf16[1,2,80,2240]{3,2,0,1:T(8,128)(2,1)}), bf16[1,4,80,2240]{3,2,0,1:T(8,128)(2,1)}) %all-gather.6.cloned.1.call-update) | async-done | bytes 1433616 | tf_op jit(solution)/shard_map/all_gather | solution.py:37
  37.7 9.3 %fusion.3 = bf16[3,1,4,80,896]{4,3,2,0,1:T(8,128)(2,1)S(1)} fusion(bf16[3,896,2240]{2,1,0:T(8,128)(2,1)} %reshape.65, bf16[1,4,80,2240]{3,2,0,1:T(8,128)(2,1)} %all-gather.6.cloned.1.call-done), kind=kOutput, calls=%fused_computation.6 | convolution fusion | flops 3853516800 | bytes 15196160 | tf_op jit(solution)/shard_map/frcd,sed->sfrce/dot_general | solution.py:35
  47.0 0.1 fusion.9
  47.1 0.2 convert_reduce_fusion
  47.3 0.8 reshape_squeeze.10
  48.1 0.0 copy-start.1
  48.1 0.8 reshape_squeeze.9
  48.8 1.2 fusion.11
  50.0 0.0 all-gather.8.cloned.1.call-update
  50.1 0.0 all-gather.10.cloned.1.call-start
  50.1 0.0 copy-done.1
  50.1 8.7 %all_gather.26 = bf16[1792,140]{0,1:T(8,128)(2,1)} all-gather(bf16[896,140]{0,1:T(8,128)(2,1)S(1)} %copy-done.1), channel_id=1, replica_groups=mesh['frames'=16,'heads'=2] {'heads'}, dimensions={0}, use_global_device_ids=true | all-gather | bytes 752640 | tf_op jit(solution)/shard_map/all_gather | solution.py:61
  58.9 0.0 all-gather.10.cloned.1.call-update
  58.9 0.1 all_gather.24
  59.0 0.1 reduce_sum.12
  59.0 0.8 reshape_squeeze.11
  59.8 21.7 %all_gather.25 = f32[16,8,112]{2,1,0:T(8,128)S(1)} all-gather(f32[1,8,112]{2,1,0:T(8,128)S(1)} %all_gather.24), channel_id=1, replica_groups=mesh['frames'=16,'heads'=2] {'frames'}, dimensions={0}, use_global_device_ids=true | all-gather | bytes 60928 | tf_op jit(solution)/shard_map/all_gather | solution.py:14
  81.5 37.3 %all-gather.8.cloned.1.call-done = f32[128,112,112]{2,1,0:T(8,128)} async-done(((f32[8,112,112]{2,1,0:T(8,128)}), f32[128,112,112]{2,1,0:T(8,128)}) %all-gather.8.cloned.1.call-update) | async-done | bytes 6422544 | tf_op jit(solution)/shard_map/all_gather | solution.py:14
  118.9 0.0 copy-start
  118.9 0.7 fusion.14
  119.6 0.3 copy-done
  119.9 0.8 fusion.8
  120.7 0.4 copy.19
  121.1 0.6 reshape.67
  121.7 12.3 %all_to_all.15 = bf16[1,4,80,896]{3,2,0,1:T(8,128)(2,1)S(1)} all-to-all(bf16[1,4,80,896]{3,2,0,1:T(8,128)(2,1)S(1)} %bitcast.64), channel_id=1, replica_groups=mesh['frames'=16,'heads'=2] {'heads'}, dimensions={1} | all-to-all | bytes 1146880 | tf_op jit(solution)/shard_map/all_to_all | solution.py:60
  134.0 0.4 copy.21
  134.5 0.4 reshape.68
  134.8 58.8 %all-gather.10.cloned.1.call-done = bf16[16,140,1792]{2,1,0:T(8,128)(2,1)} async-done(((bf16[1,140,1792]{2,1,0:T(8,128)(2,1)}), bf16[16,140,1792]{2,1,0:T(8,128)(2,1)}) %all-gather.10.cloned.1.call-update) | async-done | bytes 8028176 | tf_op jit(solution)/shard_map/all_gather | solution.py:65
  193.6 9.3 %reshape.76 = bf16[2240,1792,1]{1,0,2:T(8,128)(2,1)} reshape(bf16[16,140,1792]{2,1,0:T(8,128)(2,1)} %all-gather.10.cloned.1.call-done) | data formatting | bytes 16056320
  203.0 6.8 %fusion.2 = bf16[1,2,80,2240]{3,2,1,0:T(8,128)(2,1)} fusion(bf16[2,80,1792]{2,1,0:T(8,128)(2,1)S(1)} %reshape.68, bf16[2240,1792,1]{1,0,2:T(8,128)(2,1)} %reshape.76), kind=kOutput, calls=%fused_computation.5 | convolution fusion | flops 1284864000 | bytes 9318400 | tf_op jit(solution)/shard_map/frce,ed->frcd/dot_general | solution.py:62
  (5 shorter events, 0.1 us)
Async XLA Ops:
  6.5 31.2 %all-gather.6.cloned.1.call-start = ((), (), s32[]{:S(2)}) async-start(), calls=%async_computation.1 | async-start | bytes 2211840 | tf_op jit(solution)/shard_map/all_gather | solution.py:37
  7.3 111.6 %all-gather.8.cloned.1.call-start = ((), (), s32[]{:S(2)}) async-start(), calls=%async_computation.2 | async-start | bytes 7798784 | tf_op jit(solution)/shard_map/all_gather | solution.py:14
  48.1 2.0 copy-start.1
  50.1 143.6 %all-gather.10.cloned.1.call-start = ((), (), s32[]{:S(2)}) async-start(), calls=%async_computation.3 | async-start | bytes 8773632 | tf_op jit(solution)/shard_map/all_gather | solution.py:65
  118.9 1.0 copy-start
Sparse Core Ops, SparseCore 0:
  8.9 28.7 all-gather.5
  50.2 68.6 all-gather.7
  121.1 72.4 all-gather.9
where the time goes:
time: 218 us; the launch traced here: 216 us
  waiting for transfers between devices  108 us (50%)
  blocking collectives  42.8 us (20%)
  local copies, waits for them, and re-layouts  33.3 us (15%)
  matrix products  18.8 us (9%)
  between operations  13.2 us (6%)
    all_gather x1, waiting for transfers between devices, on_device(): lax.all_gather(full_rows, 'frames', axis=1, tiled=True)  58.8 us
    all_gather x1, waiting for transfers between devices, carried_in(): gathered = jax.tree.map(lambda a: lax.all_gather(a, axis), part)  37.3 us
    all_gather x1, blocking collectives, carried_in(): gathered = jax.tree.map(lambda a: lax.all_gather(a, axis), part)  21.7 us
    reshape x1, local copies, waits for them, and re-layouts, on_device(): weights = qkv_weight.reshape(3, local_width, feature_count)  19.5 us
    all_to_all x1, blocking collectives, on_device(): lax.all_to_all(attended, 'heads', split_axis=1, concat_axis=3, tiled=True)  12.3 us
    all_gather x1, waiting for transfers between devices, on_device(): lax.all_gather(frames_x, 'heads', axis=1, tiled=True)  10.9 us
    unnamed x5, local copies, waits for them, and re-layouts  9.57 us
    dot_general x1, matrix products, on_device(): jnp.einsum('frcd,sed->sfrce', lax.all_gather(frames_x, 'heads', axis=1, t...  9.28 us
  transfers between devices with their start and end apart: 3, of which 3 were waited for; matrix products, arithmetic and copies ran while one was open for 11% of the time, Pallas kernels for 0%

commit v1 on v0

--- a/solution.py
+++ b/solution.py
@@ -1,6 +1,10 @@
+import functools
+
 import jax
 import jax.numpy as jnp
 from jax import lax
+from jax.experimental import pallas as pl
+from jax.experimental.pallas import tpu as pltpu
 from jax.sharding import PartitionSpec as P
 
 HD = 112
@@ -68,9 +72,309 @@
     return result.astype(jnp.bfloat16)
 
 
+MESH = pl.DeviceIdType.MESH
+NT = (((1,), (1,)), ((), ()))
+TN = (((0,), (0,)), ((), ()))
+F32 = jnp.float32
+BF16 = jnp.bfloat16
+PLANES = 4
+
+
+def dot(a, b, dims):
+    return lax.dot_general(a, b, dims, preferred_element_type=F32)
+
+
+def kernel(
+    x_ref, w_ref, wo_ref, out_ref,
+    xv, xp, xe, xo, wv, wov, wog, qs, ks, vs, st, stb, cst, yb, yst, zb, zst, pb, pst, cum,
+    att, po, pin, acc,
+    lsem, x_send, x_recv, w_send, w_recv, s_send, s_recv, p_send, p_recv,
+):
+    frame = lax.axis_index("frames")
+    side = lax.axis_index("heads")
+    core = frame % 2
+    y = (frame // 2) % 2
+    z = frame // 4
+    rows, d = x_ref.shape
+    half_rows = w_ref.shape[1]
+    width = wo_ref.shape[0]
+    cols = wo_ref.shape[1]
+    block = wog.shape[1]
+    wide = xe.shape[1]
+    heads = width // HD
+    sub = HD // 2
+    pad = wide - d
+    lanes = st.shape[1] // 2
+
+    x_peer = (frame, 1 - side)
+    core_peer = (frame + 1 - 2 * core, side)
+    y_peer = (frame + 2 - 4 * y, side)
+
+    def z_peer(step):
+        return ((frame + 4 * step) % (4 * PLANES), side)
+
+    peers = [x_peer, core_peer, y_peer] + [z_peer(k) for k in range(1, PLANES)]
+
+    load_wo = pltpu.make_async_copy(wo_ref, wov, lsem.at[0])
+    load_x = pltpu.make_async_copy(x_ref, xv, lsem.at[1])
+    load_w = [pltpu.make_async_copy(w_ref.at[s], wv.at[s], lsem.at[2 + s]) for s in range(3)]
+
+    barrier = pltpu.get_barrier_semaphore()
+    for peer in peers:
+        pl.semaphore_signal(barrier, inc=1, device_id=peer, device_id_type=MESH)
+    load_wo.start()
+    load_x.start()
+    for s in (1, 2, 0):
+        load_w[s].start()
+    pl.semaphore_wait(barrier, len(peers))
+
+    def remote(src, dst, send, recv, peer):
+        return pltpu.make_async_remote_copy(
+            src_ref=src, dst_ref=dst, send_sem=send, recv_sem=recv,
+            device_id=peer, device_id_type=MESH,
+        )
+
+    parts = xp.shape[0] // CHUNK
+    x_copies = []
+    for k in range(parts):
+        span = pl.ds(k * CHUNK, CHUNK)
+        c = remote(x_ref.at[span], xp.at[span], x_send.at[k], x_recv.at[k], x_peer)
+        c.start()
+        x_copies.append(c)
+
+    load_wo.wait()
+    row = lax.broadcasted_iota(jnp.int32, (width, width), 0)
+    col = lax.broadcasted_iota(jnp.int32, (width, width), 1)
+    target = jnp.where(col < half_rows, 2 * col, 2 * (col - half_rows) + 1)
+    order = jnp.where(row == target, 1.0, 0.0).astype(BF16)
+    wog[frame, pl.ds(0, cols), :] = dot(wov[...], order, TN).astype(BF16)
+
+    wog[frame, pl.ds(cols, block - cols), :] = jnp.zeros((block - cols, width), BF16)
+    w_copies = []
+
+    def send_block(which, peer, slot):
+        c = remote(wog.at[which], wog.at[which], w_send.at[slot], w_recv.at[which], peer)
+        c.start()
+        w_copies.append(c)
+
+    def wait_block(which):
+        remote(wog.at[which], wog.at[which], w_send.at[0], w_recv.at[which], core_peer).wait_recv()
+
+    for k in range(1, PLANES):
+        send_block(frame, z_peer(k), k - 1)
+    send_block(frame, y_peer, 3)
+    send_block(frame, core_peer, 4)
+
+    def place(src, at, count, start):
+        xe[start : start + count, 0:d] = src[at : at + count, :]
+        xe[start : start + count, d:wide] = jnp.zeros((count, pad), BF16)
+        xo[start : start + count, pad:wide] = src[at : at + count, :]
+        xo[start : start + count, 0:pad] = jnp.zeros((count, pad), BF16)
+
+    def project(s, dst, start, count, relu):
+        for j, (src, lo) in enumerate(((xe, 0), (xo, d - pad))):
+            p = dot(src[start : start + count, :], wv[s, :, lo : lo + wide], NT)
+            if relu:
+                p = jnp.maximum(p, 0.0)
+            dst[start : start + count, j * lanes : j * lanes + half_rows] = p.astype(BF16)
+
+    total = qs.shape[0]
+    vs[:, half_rows:lanes] = jnp.ones((total, lanes - half_rows), BF16)
+    vs[:, lanes + half_rows : 2 * lanes] = jnp.zeros((total, lanes - half_rows), BF16)
+
+    load_x.wait()
+    place(xv, 0, rows, 0)
+    load_w[1].wait()
+    project(1, ks, 0, rows, True)
+    load_w[2].wait()
+    project(2, vs, 0, rows, False)
+
+    y_own = 4 * z + 2 * (1 - y) + core
+
+    def forward_z(k):
+        which = (frame + 4 * (PLANES - k)) % (4 * PLANES)
+        wait_block(which)
+        send_block(which, y_peer, 5 + 2 * k)
+        send_block(which, core_peer, 6 + 2 * k)
+
+    wait_block(y_own)
+    send_block(y_own, core_peer, 5)
+
+    load_w[0].wait()
+    project(0, qs, 0, rows, True)
+
+    for k in range(parts):
+        x_copies[k].wait_recv()
+        place(xp, k * CHUNK, CHUNK, rows + k * CHUNK)
+        project(1, ks, rows + k * CHUNK, CHUNK, True)
+        project(2, vs, rows + k * CHUNK, CHUNK, False)
+
+    srow = lax.broadcasted_iota(jnp.int32, (half_rows, lanes), 0) // sub
+    scol = lax.broadcasted_iota(jnp.int32, (half_rows, lanes), 1)
+    mask = srow == jnp.where(scol < half_rows, scol // sub, scol - half_rows)
+
+    for i in range(2):
+        for j in range(2):
+            full = dot(
+                ks[:, i * lanes : i * lanes + half_rows],
+                vs[:, j * lanes : (j + 1) * lanes],
+                TN,
+            )
+            full = jnp.where(mask, full, 0.0)
+            small = full[0:sub]
+            for h in range(1, heads):
+                small = small + full[h * sub : (h + 1) * sub]
+            st[i * sub : (i + 1) * sub, j * lanes : (j + 1) * lanes] = small
+    stb[...] = st[...].astype(BF16)
+    c_core = remote(stb, cst, s_send.at[0], s_recv.at[0], core_peer)
+    c_core.start()
+    c_core.wait_recv()
+
+    mine = pl.ds(pl.multiple_of(core * lanes, 128), lanes)
+    other = pl.ds(pl.multiple_of((1 - core) * lanes, 128), lanes)
+    pair = st[:, mine] + cst[:, mine].astype(F32)
+    yb[...] = pair.astype(BF16)
+    c_y = remote(yb, yst, s_send.at[1], s_recv.at[1], y_peer)
+    c_y.start()
+    c_y.wait_recv()
+    zb[...] = (pair + yst[...].astype(F32)).astype(BF16)
+
+    for k in range(1, PLANES):
+        @pl.when(z + k < PLANES)
+        def _():
+            remote(zb, zst.at[k - 1], s_send.at[1 + k], s_recv.at[1 + k], z_peer(k)).start()
+
+    for k in range(1, PLANES):
+        forward_z(k)
+
+    project(0, qs, rows, rows, True)
+
+    cum[...] = st[...] + cst[...].astype(F32) * core.astype(F32)
+    prior = yst[...].astype(F32) * y.astype(F32)
+    pb[...] = prior.astype(BF16)
+    acc[0:HD, 0:lanes] = prior
+    for k in range(1, PLANES):
+        @pl.when(z >= k)
+        def _():
+            remote(zb, zst.at[k - 1], s_send.at[1 + k], s_recv.at[1 + k], z_peer(k)).wait_recv()
+            acc[0:HD, 0:lanes] += zst[k - 1].astype(F32)
+    pb[...] = acc[0:HD, 0:lanes].astype(BF16)
+    c_p = remote(pb, pst, s_send.at[1 + PLANES], s_recv.at[1 + PLANES], core_peer)
+    c_p.start()
+    cum[:, mine] += acc[0:HD, 0:lanes]
+    c_p.wait_recv()
+    cum[:, other] += pst[...].astype(F32)
+
+    nums = []
+    for j in range(2):
+        num = None
+        for i in range(2):
+            part = cum[i * sub : (i + 1) * sub, j * lanes : (j + 1) * lanes]
+            full = jnp.where(mask, jnp.concatenate([part] * heads, axis=0), 0.0).astype(BF16)
+            t = dot(
+                qs[:, i * lanes : i * lanes + half_rows], full, (((1,), (0,)), ((), ()))
+            )
+            num = t if num is None else num + t
+        nums.append(num)
+    den = nums[0][:, lanes - 128 : lanes]
+    at = half_rows - (lanes - 128)
+    lane = lax.broadcasted_iota(jnp.int32, den.shape, 1)
+    live = (lane >= at) & (lane < at + heads)
+    inv = jnp.where(live, 1.0 / (jnp.where(live, den, 1.0) + EPSILON), 0.0)
+    high = inv.astype(BF16)
+    low = (inv - high.astype(F32)).astype(BF16)
+    erow = lax.broadcasted_iota(jnp.int32, (128, lanes), 0) - at
+    ecol = lax.broadcasted_iota(jnp.int32, (128, lanes), 1)
+    spread = jnp.where((ecol < half_rows) & (erow == ecol // sub), 1.0, 0.0).astype(BF16)
+    nn = (((1,), (0,)), ((), ()))
+    scale = dot(high, spread, nn) + dot(low, spread, nn)
+    for j in range(2):
+        a = (nums[j] * scale).astype(BF16)
+        att[:, j * half_rows : (j + 1) * half_rows] = a[:, 0:half_rows]
+
+    for k in range(1, PLANES):
+        which = (y_own + 4 * k) % (4 * PLANES)
+        wait_block(which)
+        send_block(which, core_peer, 12 + k)
+    for zz in range(PLANES):
+        for yy in range(2):
+            wait_block(4 * zz + 2 * yy + 1 - core)
+
+    per = block * wog.shape[0] // TILES
+    step = per // 256
+    blocks = wog.shape[0] // TILES
+
+    def tile(t):
+        return jnp.concatenate([wog[t * blocks + b] for b in range(blocks)], axis=0)
+
+    p_copies = []
+    for t in range(TILES):
+        span = pl.ds(t * per, per)
+        po[:, t * per : (t + 1) * per] = dot(att[rows : 2 * rows, :], tile(t), NT).astype(BF16)
+        c = remote(po.at[:, span], pin.at[:, span], p_send.at[t], p_recv.at[t], x_peer)
+        c.start()
+        p_copies.append(c)
+    for t in range(TILES):
+        acc[:, t * per : (t + 1) * per] = dot(att[0:rows, :], tile(t), NT)
+    for t in range(TILES):
+        p_copies[t].wait_recv()
+        a = acc[:, t * per : (t + 1) * per] + pin[:, t * per : (t + 1) * per].astype(F32)
+        out_ref[:, t * per : (t + 1) * per] = a.astype(BF16)
+
+    for c in x_copies + w_copies + [c_core, c_y, c_p] + p_copies:
+        c.wait_send()
+    for k in range(1, PLANES):
+        @pl.when(z + k < PLANES)
+        def _():
+            remote(zb, zst.at[k - 1], s_send.at[1 + k], s_recv.at[1 + k], z_peer(k)).wait_send()
+
+
+CHUNK = 80
+TILES = 2
+
+
+def fused(frames_x, qkv_weight, out_weight):
+    _, row_count, col_count, d = frames_x.shape
+    rows = row_count * col_count
+    half_rows = qkv_weight.shape[1]
+    width, cols = out_weight.shape
+    frames = 4 * PLANES
+    block = -(-cols // 16) * 16
+    wide = -(-d // 256) * 256
+    lanes = 512
+    any_space = pl.BlockSpec(memory_space=pl.ANY)
+    dma = pltpu.SemaphoreType.DMA
+    v = pltpu.VMEM
+    out = pl.pallas_call(
+        kernel,
+        out_shape=jax.ShapeDtypeStruct((rows, frames * block), BF16),
+        in_specs=[any_space] * 3,
+        out_specs=pl.BlockSpec(memory_space=pltpu.VMEM),
+        scratch_shapes=[
+            v((rows, d), BF16), v((rows, d), BF16), v((2 * rows, wide), BF16), v((2 * rows, wide), BF16),
+            v(qkv_weight.shape, BF16), v((width, cols), BF16), v((frames, block, width), BF16),
+            v((2 * rows, 2 * lanes), BF16), v((2 * rows, 2 * lanes), BF16), v((2 * rows, 2 * lanes), BF16),
+            v((HD, 2 * lanes), F32), v((HD, 2 * lanes), BF16), v((HD, 2 * lanes), BF16),
+            v((HD, lanes), BF16), v((HD, lanes), BF16), v((HD, lanes), BF16),
+            v((PLANES - 1, HD, lanes), BF16), v((HD, lanes), BF16), v((HD, lanes), BF16),
+            v((HD, 2 * lanes), F32),
+            v((2 * rows, width), BF16), v((rows, frames * block), BF16), v((rows, frames * block), BF16),
+            v((rows, frames * block), F32),
+            dma((5,)), dma((rows // CHUNK,)), dma((rows // CHUNK,)), dma((16,)), dma((frames,)),
+            dma((2 + PLANES,)), dma((2 + PLANES,)), dma((TILES,)), dma((TILES,)),
+        ],
+        compiler_params=pltpu.CompilerParams(
+            collective_id=0, has_side_effects=True, vmem_limit_bytes=56 * 2**20
+        ),
+    )(frames_x.reshape(rows, d), qkv_weight, out_weight)
+    out = out.reshape(rows, frames, block)[:, :, :cols]
+    return out.reshape(1, row_count, col_count, d)
+
+
 def solution(mesh):
     in_specs = (P("frames", "heads", None, None), P(None, "heads", None), P("heads", "frames"))
     out_specs = P("frames", "heads", None, None)
+    small = mesh.shape["frames"] == 4 * PLANES and mesh.shape["heads"] == 2
     return jax.shard_map(
-        on_device, mesh=mesh, in_specs=in_specs, out_specs=out_specs, check_vma=False
-    )
+        fused if small else on_device, mesh=mesh, in_specs=in_specs, out_specs=out_specs, check_vma=False
+    )

time: 218 us -> 80.1 us (0.37)
  waiting for transfers between devices: 108 us -> 0 us
  Pallas kernels: 0 us -> 71.7 us
  blocking collectives: 42.8 us -> 0 us
  local copies, waits for them, and re-layouts: 33.3 us -> 8.22 us
  matrix products: 18.8 us -> 0 us
  between operations: 13.2 us -> 0.02 us
    all_gather x3 -> x0, waiting for transfers between devices: 107 us -> none  [the longest x1 58.8 us: on_device(): lax.all_gather(full_rows, 'frames', axis=1, tiled=True)]
    pallas_call x0 -> x1, Pallas kernels: none -> 71.7 us  [fused(): pl.pallas_call(kernel, out_shape=jax.ShapeDtypeStruct((rows, frames * blo...]
    all_gather x2 -> x0, blocking collectives: 30.5 us -> none  [the longest x1 21.7 us: carried_in(): gathered = jax.tree.map(lambda a: lax.all_gather(a, axis), part)]
    dot_general x5 -> x0, matrix products: 18.8 us -> none  [the longest x1 9.28 us: on_device(): jnp.einsum('frcd,sed->sfrce', lax.all_gather(frames_x, 'heads', axis=1, t...]
    reshape x2, local copies, waits for them, and re-layouts: 20.1 us -> 6.3 us  [the longest x1 3.18 us: fused(): out = out.reshape(rows, frames, block)[:, :, :cols]]
    all_to_all x1 -> x0, blocking collectives: 12.3 us -> none  [on_device(): lax.all_to_all(attended, 'heads', split_axis=1, concat_axis=3, tiled=True)]
    unnamed x5 -> x1, local copies, waits for them, and re-layouts: 9.57 us -> 1.92 us
    another operation x4 -> x0, local copies, waits for them, and re-layouts: 2.64 us -> none  [the longest x1 0.76 us: on_device(): query = projected[0].reshape(tokens, head_count, HD)]
  transfers between devices with their start and end apart: 3 -> 0, of which waited for: 3 -> 0; matrix products, arithmetic and copies ran while one was open for 11% -> 0% of each run, Pallas kernels for 0% -> 0%
where the time goes in v1:
time: 80.1 us; the launch traced here: 79.9 us
  Pallas kernels  71.7 us (90%)
  local copies, waits for them, and re-layouts  8.22 us (10%)
    pallas_call x1, Pallas kernels, fused(): pl.pallas_call(kernel, out_shape=jax.ShapeDtypeStruct((rows, frames * blo...  71.7 us
    reshape x1, local copies, waits for them, and re-layouts, fused(): out = out.reshape(rows, frames, block)[:, :, :cols]  3.18 us
    reshape x1, local copies, waits for them, and re-layouts, fused(): return out.reshape(1, row_count, col_count, d)  3.13 us
    unnamed x1, local copies, waits for them, and re-layouts  1.92 us

profile of v1, /device:TPU:0, one launch (start us, length us, event | category | flops | bytes accessed | tf_op | source)
XLA Modules:
  0.0 79.9 jit_solution(13127625981465834955)
XLA Ops:
  0.0 1.9 %copy.5.wo_ref = bf16[896,140]{1,0:T(8,128)(2,1)} copy(bf16[896,140]{0,1:T(8,128)(2,1)} %param.5) | data formatting | bytes 501760 | tf_op args[2]
  1.9 71.7 %shard_map.37 = bf16[160,2304]{1,0:T(8,128)(2,1)} custom-call(bf16[160,2240]{1,0:T(8,128)(2,1)} %bitcast.3, bf16[3,448,4480]{2,1,0:T(8,128)(2,1)} %w_ref.1, bf16[896,140]{1,0:T(8,128)(2,1)} %copy.5.wo_ref), custom_call_target="tpu_custom_call" | custom-call | tf_op jit(solution)/shard_map/pallas_call | solution.py:348
  73.6 3.2 %reshape.10 = bf16[160,16,144]{2,1,0:T(8,128)(2,1)S(1)} reshape(bf16[160,2304]{1,0:T(8,128)(2,1)} %shard_map.37) | data formatting | bytes 1474560 | tf_op jit(solution)/shard_map/reshape | solution.py:370
  76.8 3.1 %reshape.11 = bf16[1,2,80,2240]{3,2,1,0:T(8,128)(2,1)} reshape(bf16[160,16,140]{2,1,0:T(8,128)(2,1)S(1)} %bitcast.2) | data formatting | bytes 1433600 | tf_op jit(solution)/shard_map/reshape | solution.py:371

commit v2 on v1

--- a/solution.py
+++ b/solution.py
@@ -75,6 +75,7 @@
 MESH = pl.DeviceIdType.MESH
 NT = (((1,), (1,)), ((), ()))
 TN = (((0,), (0,)), ((), ()))
+NN = (((1,), (0,)), ((), ()))
 F32 = jnp.float32
 BF16 = jnp.bfloat16
 PLANES = 4
@@ -97,8 +98,7 @@
     z = frame // 4
     rows, d = x_ref.shape
     half_rows = w_ref.shape[1]
-    width = wo_ref.shape[0]
-    cols = wo_ref.shape[1]
+    cols, width = wo_ref.shape
     block = wog.shape[1]
     wide = xe.shape[1]
     heads = width // HD
@@ -147,7 +147,7 @@
     col = lax.broadcasted_iota(jnp.int32, (width, width), 1)
     target = jnp.where(col < half_rows, 2 * col, 2 * (col - half_rows) + 1)
     order = jnp.where(row == target, 1.0, 0.0).astype(BF16)
-    wog[frame, pl.ds(0, cols), :] = dot(wov[...], order, TN).astype(BF16)
+    wog[frame, pl.ds(0, cols), :] = dot(wov[...], order, NN).astype(BF16)
 
     wog[frame, pl.ds(cols, block - cols), :] = jnp.zeros((block - cols, width), BF16)
     w_copies = []
@@ -272,7 +272,7 @@
             part = cum[i * sub : (i + 1) * sub, j * lanes : (j + 1) * lanes]
             full = jnp.where(mask, jnp.concatenate([part] * heads, axis=0), 0.0).astype(BF16)
             t = dot(
-                qs[:, i * lanes : i * lanes + half_rows], full, (((1,), (0,)), ((), ()))
+                qs[:, i * lanes : i * lanes + half_rows], full, NN
             )
             num = t if num is None else num + t
         nums.append(num)
@@ -286,8 +286,7 @@
     erow = lax.broadcasted_iota(jnp.int32, (128, lanes), 0) - at
     ecol = lax.broadcasted_iota(jnp.int32, (128, lanes), 1)
     spread = jnp.where((ecol < half_rows) & (erow == ecol // sub), 1.0, 0.0).astype(BF16)
-    nn = (((1,), (0,)), ((), ()))
-    scale = dot(high, spread, nn) + dot(low, spread, nn)
+    scale = dot(high, spread, NN) + dot(low, spread, NN)
     for j in range(2):
         a = (nums[j] * scale).astype(BF16)
         att[:, j * half_rows : (j + 1) * half_rows] = a[:, 0:half_rows]
@@ -301,7 +300,6 @@
             wait_block(4 * zz + 2 * yy + 1 - core)
 
     per = block * wog.shape[0] // TILES
-    step = per // 256
     blocks = wog.shape[0] // TILES
 
     def tile(t):
@@ -319,7 +317,9 @@
     for t in range(TILES):
         p_copies[t].wait_recv()
         a = acc[:, t * per : (t + 1) * per] + pin[:, t * per : (t + 1) * per].astype(F32)
-        out_ref[:, t * per : (t + 1) * per] = a.astype(BF16)
+        for b in range(blocks):
+            f = t * blocks + b
+            out_ref[:, f * cols : (f + 1) * cols] = a[:, b * block : b * block + cols].astype(BF16)
 
     for c in x_copies + w_copies + [c_core, c_y, c_p] + p_copies:
         c.wait_send()
@@ -347,12 +347,12 @@
     v = pltpu.VMEM
     out = pl.pallas_call(
         kernel,
-        out_shape=jax.ShapeDtypeStruct((rows, frames * block), BF16),
+        out_shape=jax.ShapeDtypeStruct((rows, d), BF16),
         in_specs=[any_space] * 3,
         out_specs=pl.BlockSpec(memory_space=pltpu.VMEM),
         scratch_shapes=[
             v((rows, d), BF16), v((rows, d), BF16), v((2 * rows, wide), BF16), v((2 * rows, wide), BF16),
-            v(qkv_weight.shape, BF16), v((width, cols), BF16), v((frames, block, width), BF16),
+            v(qkv_weight.shape, BF16), v((cols, width), BF16), v((frames, block, width), BF16),
             v((2 * rows, 2 * lanes), BF16), v((2 * rows, 2 * lanes), BF16), v((2 * rows, 2 * lanes), BF16),
             v((HD, 2 * lanes), F32), v((HD, 2 * lanes), BF16), v((HD, 2 * lanes), BF16),
             v((HD, lanes), BF16), v((HD, lanes), BF16), v((HD, lanes), BF16),
@@ -366,8 +366,7 @@
         compiler_params=pltpu.CompilerParams(
             collective_id=0, has_side_effects=True, vmem_limit_bytes=56 * 2**20
         ),
-    )(frames_x.reshape(rows, d), qkv_weight, out_weight)
-    out = out.reshape(rows, frames, block)[:, :, :cols]
+    )(frames_x.reshape(rows, d), qkv_weight, out_weight.T)
     return out.reshape(1, row_count, col_count, d)
 
 

time: 80.1 us -> 74 us (0.924)
  local copies, waits for them, and re-layouts: 8.22 us -> 2.03 us
    reshape x2 -> x0, local copies, waits for them, and re-layouts: 6.3 us -> none  [the longest x1 3.18 us: fused(): out = out.reshape(rows, frames, block)[:, :, :cols]]
where the time goes in v2:
time: 74 us; the launch traced here: 73.9 us
  Pallas kernels  71.8 us (97%)
  local copies, waits for them, and re-layouts  2.03 us (3%)
    pallas_call x1, Pallas kernels, fused(): pl.pallas_call(kernel, out_shape=jax.ShapeDtypeStruct((rows, d), BF16), i...  71.8 us
    unnamed x1, local copies, waits for them, and re-layouts  2.03 us

profile of v2, /device:TPU:0, one launch (start us, length us, event | category | flops | bytes accessed | tf_op | source)
XLA Modules:
  0.0 73.9 jit_solution(13707756872778324674)
XLA Ops:
  0.0 71.8 %shard_map.37 = bf16[160,2240]{1,0:T(8,128)(2,1)} custom-call(bf16[160,2240]{1,0:T(8,128)(2,1)} %bitcast.4, bf16[3,448,4480]{2,1,0:T(8,128)(2,1)} %w_ref.1, bf16[140,896]{1,0:T(8,128)(2,1)} %bitcast.5), custom_call_target="tpu_custom_call" | custom-call | tf_op jit(solution)/shard_map/pallas_call | solution.py:348
  71.9 2.0 %copy.5 = bf16[1,2,80,2240]{3,2,1,0:T(8,128)(2,1)} copy(bf16[1,2,80,2240]{3,2,1,0:T(8,128)(2,1)} %bitcast.3) | data formatting | bytes 1433600

commit v3 on v2

--- a/solution.py
+++ b/solution.py
@@ -88,7 +88,7 @@
 def kernel(
     x_ref, w_ref, wo_ref, out_ref,
     xv, xp, xe, xo, wv, wov, wog, qs, ks, vs, st, stb, cst, yb, yst, zb, zst, pb, pst, cum,
-    att, po, pin, acc,
+    big, att, po, pin, acc,
     lsem, x_send, x_recv, w_send, w_recv, s_send, s_recv, p_send, p_recv,
 ):
     frame = lax.axis_index("frames")
@@ -99,7 +99,7 @@
     rows, d = x_ref.shape
     half_rows = w_ref.shape[1]
     cols, width = wo_ref.shape
-    block = wog.shape[1]
+    block = wog.shape[0] // (4 * PLANES)
     wide = xe.shape[1]
     heads = width // HD
     sub = HD // 2
@@ -147,23 +147,52 @@
     col = lax.broadcasted_iota(jnp.int32, (width, width), 1)
     target = jnp.where(col < half_rows, 2 * col, 2 * (col - half_rows) + 1)
     order = jnp.where(row == target, 1.0, 0.0).astype(BF16)
-    wog[frame, pl.ds(0, cols), :] = dot(wov[...], order, NN).astype(BF16)
-
-    wog[frame, pl.ds(cols, block - cols), :] = jnp.zeros((block - cols, width), BF16)
-    w_copies = []
-
-    def send_block(which, peer, slot):
-        c = remote(wog.at[which], wog.at[which], w_send.at[slot], w_recv.at[which], peer)
-        c.start()
-        w_copies.append(c)
-
-    def wait_block(which):
-        remote(wog.at[which], wog.at[which], w_send.at[0], w_recv.at[which], core_peer).wait_recv()
-
-    for k in range(1, PLANES):
-        send_block(frame, z_peer(k), k - 1)
-    send_block(frame, y_peer, 3)
-    send_block(frame, core_peer, 4)
+    own = dot(wov[...], order, NN).astype(BF16)
+    wog[pl.ds(pl.multiple_of(frame * block, 16), block), :] = jnp.concatenate(
+        [own, jnp.zeros((block - cols, width), BF16)], axis=0
+    )
+    sent = []
+
+    def rows_of(which):
+        return wog.at[pl.ds(pl.multiple_of(which * block, 16), block)]
+
+    def send_block(which, peer, slot, *conds):
+        c = remote(rows_of(which), rows_of(which), w_send.at[slot], w_recv.at[which], peer)
+        under(conds, c.start)
+        sent.append((conds, c))
+
+    def under(conds, act):
+        if not conds:
+            act()
+            return
+        cond = conds[0]
+        for extra in conds[1:]:
+            cond = cond & extra
+        pl.when(cond)(act)
+
+    def wait_block(which, *conds):
+        c = remote(rows_of(which), rows_of(which), w_send.at[0], w_recv.at[which], core_peer)
+        under(conds, c.wait_recv)
+
+    down, up = z_peer(PLANES - 1), z_peer(1)
+    has_down, has_up = z > 0, z < PLANES - 1
+    send_block(frame, down, 0, has_down)
+    send_block(frame, up, 1, has_up)
+    send_block(frame, y_peer, 2)
+    send_block(frame, core_peer, 3)
+
+    def pass_on(k):
+        below = (frame + 4 * (PLANES - k)) % (4 * PLANES)
+        above = (frame + 4 * k) % (4 * PLANES)
+        for j, (which, there, onward, more) in enumerate(
+            ((below, z >= k, up, has_up), (above, z + k < PLANES, down, has_down))
+        ):
+            slot = 4 + 6 * (k - 1) + 3 * j
+            wait_block(which, there)
+            if k < PLANES - 1:
+                send_block(which, onward, slot, there, more)
+            send_block(which, y_peer, slot + 1, there)
+            send_block(which, core_peer, slot + 2, there)
 
     def place(src, at, count, start):
         xe[start : start + count, 0:d] = src[at : at + count, :]
@@ -191,40 +220,38 @@
 
     y_own = 4 * z + 2 * (1 - y) + core
 
-    def forward_z(k):
-        which = (frame + 4 * (PLANES - k)) % (4 * PLANES)
-        wait_block(which)
-        send_block(which, y_peer, 5 + 2 * k)
-        send_block(which, core_peer, 6 + 2 * k)
-
+    srow = lax.broadcasted_iota(jnp.int32, (half_rows, lanes), 0) // sub
+    scol = lax.broadcasted_iota(jnp.int32, (half_rows, lanes), 1)
+    mask = srow == jnp.where(scol < half_rows, scol // sub, scol - half_rows)
+
+    def add_state(start, count, first):
+        for i in range(2):
+            for j in range(2):
+                full = dot(
+                    ks[start : start + count, i * lanes : i * lanes + half_rows],
+                    vs[start : start + count, j * lanes : (j + 1) * lanes],
+                    TN,
+                )
+                full = jnp.where(mask, full, 0.0)
+                small = full[0:sub]
+                for h in range(1, heads):
+                    small = small + full[h * sub : (h + 1) * sub]
+                at = (slice(i * sub, (i + 1) * sub), slice(j * lanes, (j + 1) * lanes))
+                st[at] = small if first else st[at] + small
+
+    add_state(0, rows, True)
+    pass_on(1)
     wait_block(y_own)
-    send_block(y_own, core_peer, 5)
-
+    send_block(y_own, core_peer, 22)
     load_w[0].wait()
-    project(0, qs, 0, rows, True)
-
     for k in range(parts):
         x_copies[k].wait_recv()
         place(xp, k * CHUNK, CHUNK, rows + k * CHUNK)
         project(1, ks, rows + k * CHUNK, CHUNK, True)
         project(2, vs, rows + k * CHUNK, CHUNK, False)
-
-    srow = lax.broadcasted_iota(jnp.int32, (half_rows, lanes), 0) // sub
-    scol = lax.broadcasted_iota(jnp.int32, (half_rows, lanes), 1)
-    mask = srow == jnp.where(scol < half_rows, scol // sub, scol - half_rows)
-
-    for i in range(2):
-        for j in range(2):
-            full = dot(
-                ks[:, i * lanes : i * lanes + half_rows],
-                vs[:, j * lanes : (j + 1) * lanes],
-                TN,
-            )
-            full = jnp.where(mask, full, 0.0)
-            small = full[0:sub]
-            for h in range(1, heads):
-                small = small + full[h * sub : (h + 1) * sub]
-            st[i * sub : (i + 1) * sub, j * lanes : (j + 1) * lanes] = small
+        add_state(rows + k * CHUNK, CHUNK, False)
+        if k == 0:
+            pass_on(2)
     stb[...] = st[...].astype(BF16)
     c_core = remote(stb, cst, s_send.at[0], s_recv.at[0], core_peer)
     c_core.start()
@@ -244,10 +271,8 @@
         def _():
             remote(zb, zst.at[k - 1], s_send.at[1 + k], s_recv.at[1 + k], z_peer(k)).start()
 
-    for k in range(1, PLANES):
-        forward_z(k)
-
-    project(0, qs, rows, rows, True)
+    pass_on(3)
+    project(0, qs, 0, 2 * rows, True)
 
     cum[...] = st[...] + cst[...].astype(F32) * core.astype(F32)
     prior = yst[...].astype(F32) * y.astype(F32)
@@ -265,64 +290,72 @@
     c_p.wait_recv()
     cum[:, other] += pst[...].astype(F32)
 
-    nums = []
-    for j in range(2):
-        num = None
-        for i in range(2):
-            part = cum[i * sub : (i + 1) * sub, j * lanes : (j + 1) * lanes]
-            full = jnp.where(mask, jnp.concatenate([part] * heads, axis=0), 0.0).astype(BF16)
-            t = dot(
-                qs[:, i * lanes : i * lanes + half_rows], full, NN
-            )
-            num = t if num is None else num + t
-        nums.append(num)
-    den = nums[0][:, lanes - 128 : lanes]
     at = half_rows - (lanes - 128)
-    lane = lax.broadcasted_iota(jnp.int32, den.shape, 1)
-    live = (lane >= at) & (lane < at + heads)
-    inv = jnp.where(live, 1.0 / (jnp.where(live, den, 1.0) + EPSILON), 0.0)
-    high = inv.astype(BF16)
-    low = (inv - high.astype(F32)).astype(BF16)
     erow = lax.broadcasted_iota(jnp.int32, (128, lanes), 0) - at
     ecol = lax.broadcasted_iota(jnp.int32, (128, lanes), 1)
     spread = jnp.where((ecol < half_rows) & (erow == ecol // sub), 1.0, 0.0).astype(BF16)
-    scale = dot(high, spread, NN) + dot(low, spread, NN)
-    for j in range(2):
-        a = (nums[j] * scale).astype(BF16)
-        att[:, j * half_rows : (j + 1) * half_rows] = a[:, 0:half_rows]
+    for i in range(2):
+        for j in range(2):
+            part = cum[i * sub : (i + 1) * sub, j * lanes : (j + 1) * lanes]
+            full = jnp.where(mask, jnp.concatenate([part] * heads, axis=0), 0.0).astype(BF16)
+            big[i, j] = full
+
+    def attend(start):
+        nums = []
+        for j in range(2):
+            num = None
+            for i in range(2):
+                t = dot(qs[start : start + rows, i * lanes : i * lanes + half_rows], big[i, j], NN)
+                num = t if num is None else num + t
+            nums.append(num)
+        den = nums[0][:, lanes - 128 : lanes]
+        lane = lax.broadcasted_iota(jnp.int32, den.shape, 1)
+        live = (lane >= at) & (lane < at + heads)
+        inv = jnp.where(live, 1.0 / (jnp.where(live, den, 1.0) + EPSILON), 0.0)
+        high = inv.astype(BF16)
+        low = (inv - high.astype(F32)).astype(BF16)
+        scale = dot(high, spread, NN) + dot(low, spread, NN)
+        for j in range(2):
+            a = (nums[j] * scale).astype(BF16)
+            att[start : start + rows, j * half_rows : (j + 1) * half_rows] = a[:, 0:half_rows]
+
+    attend(rows)
 
     for k in range(1, PLANES):
         which = (y_own + 4 * k) % (4 * PLANES)
         wait_block(which)
-        send_block(which, core_peer, 12 + k)
+        send_block(which, core_peer, 22 + k)
     for zz in range(PLANES):
         for yy in range(2):
             wait_block(4 * zz + 2 * yy + 1 - core)
 
-    per = block * wog.shape[0] // TILES
-    blocks = wog.shape[0] // TILES
-
-    def tile(t):
-        return jnp.concatenate([wog[t * blocks + b] for b in range(blocks)], axis=0)
-
+    per = wog.shape[0] // TILES
     p_copies = []
     for t in range(TILES):
-        span = pl.ds(t * per, per)
-        po[:, t * per : (t + 1) * per] = dot(att[rows : 2 * rows, :], tile(t), NT).astype(BF16)
-        c = remote(po.at[:, span], pin.at[:, span], p_send.at[t], p_recv.at[t], x_peer)
+        span = slice(t * per, (t + 1) * per)
+        po[:, span] = dot(att[rows : 2 * rows, :], wog[span, :], NT).astype(BF16)
+        at_cols = pl.ds(t * per, per)
+        c = remote(po.at[:, at_cols], pin.at[:, at_cols], p_send.at[t], p_recv.at[t], x_peer)
         c.start()
         p_copies.append(c)
+    attend(0)
     for t in range(TILES):
-        acc[:, t * per : (t + 1) * per] = dot(att[0:rows, :], tile(t), NT)
+        span = slice(t * per, (t + 1) * per)
+        acc[:, span] = dot(att[0:rows, :], wog[span, :], NT)
+    done = 0
     for t in range(TILES):
+        span = slice(t * per, (t + 1) * per)
         p_copies[t].wait_recv()
-        a = acc[:, t * per : (t + 1) * per] + pin[:, t * per : (t + 1) * per].astype(F32)
-        for b in range(blocks):
-            f = t * blocks + b
-            out_ref[:, f * cols : (f + 1) * cols] = a[:, b * block : b * block + cols].astype(BF16)
-
-    for c in x_copies + w_copies + [c_core, c_y, c_p] + p_copies:
+        acc[:, span] += pin[:, span].astype(F32)
+        while done < 4 * PLANES and (done + 1) * block <= (t + 1) * per:
+            piece = acc[:, done * block : done * block + cols]
+            out_ref[:, done * cols : (done + 1) * cols] = piece.astype(BF16)
+            done += 1
+
+    for c in x_copies + [c_core, c_y, c_p] + p_copies:
         c.wait_send()
+    for conds, c in sent:
+        under(conds, c.wait_send)
     for k in range(1, PLANES):
         @pl.when(z + k < PLANES)
         def _():
@@ -330,7 +363,7 @@
 
 
 CHUNK = 80
-TILES = 2
+TILES = 3
 
 
 def fused(frames_x, qkv_weight, out_weight):
@@ -352,15 +385,16 @@
         out_specs=pl.BlockSpec(memory_space=pltpu.VMEM),
         scratch_shapes=[
             v((rows, d), BF16), v((rows, d), BF16), v((2 * rows, wide), BF16), v((2 * rows, wide), BF16),
-            v(qkv_weight.shape, BF16), v((cols, width), BF16), v((frames, block, width), BF16),
+            v(qkv_weight.shape, BF16), v((cols, width), BF16), v((frames * block, width), BF16),
             v((2 * rows, 2 * lanes), BF16), v((2 * rows, 2 * lanes), BF16), v((2 * rows, 2 * lanes), BF16),
             v((HD, 2 * lanes), F32), v((HD, 2 * lanes), BF16), v((HD, 2 * lanes), BF16),
             v((HD, lanes), BF16), v((HD, lanes), BF16), v((HD, lanes), BF16),
             v((PLANES - 1, HD, lanes), BF16), v((HD, lanes), BF16), v((HD, lanes), BF16),
             v((HD, 2 * lanes), F32),
+            v((2, 2, half_rows, lanes), BF16),
             v((2 * rows, width), BF16), v((rows, frames * block), BF16), v((rows, frames * block), BF16),
             v((rows, frames * block), F32),
-            dma((5,)), dma((rows // CHUNK,)), dma((rows // CHUNK,)), dma((16,)), dma((frames,)),
+            dma((5,)), dma((rows // CHUNK,)), dma((rows // CHUNK,)), dma((26,)), dma((frames,)),
             dma((2 + PLANES,)), dma((2 + PLANES,)), dma((TILES,)), dma((TILES,)),
         ],
         compiler_params=pltpu.CompilerParams(

time: 74 us -> 66.2 us (0.89)
  the two profiles are of different devices: /device:TPU:0 before, /device:TPU:24 now
where the time goes in v3:
time: 66.2 us; the launch traced here: 66.1 us
  Pallas kernels  64.1 us (97%)
  local copies, waits for them, and re-layouts  2.03 us (3%)
    pallas_call x1, Pallas kernels, fused(): pl.pallas_call(kernel, out_shape=jax.ShapeDtypeStruct((rows, d), BF16), i...  64.1 us
    unnamed x1, local copies, waits for them, and re-layouts  2.03 us

profile of v3, /device:TPU:24, one launch (start us, length us, event | category | flops | bytes accessed | tf_op | source)
XLA Modules:
  0.0 66.1 jit_solution(10253957692845633510)
XLA Ops:
  0.0 64.1 %shard_map.37 = bf16[160,2240]{1,0:T(8,128)(2,1)} custom-call(bf16[160,2240]{1,0:T(8,128)(2,1)} %bitcast.4, bf16[3,448,4480]{2,1,0:T(8,128)(2,1)} %w_ref.1, bf16[140,896]{1,0:T(8,128)(2,1)} %bitcast.5), custom_call_target="tpu_custom_call" | custom-call | tf_op jit(solution)/shard_map/pallas_call | solution.py:381
  64.1 2.0 %copy.5 = bf16[1,2,80,2240]{3,2,1,0:T(8,128)(2,1)} copy(bf16[1,2,80,2240]{3,2,1,0:T(8,128)(2,1)} %bitcast.3) | data formatting | bytes 1433600

commit v4 on v3

--- a/solution.py
+++ b/solution.py
@@ -215,6 +215,7 @@
     place(xv, 0, rows, 0)
     load_w[1].wait()
     project(1, ks, 0, rows, True)
+    pass_on(1)
     load_w[2].wait()
     project(2, vs, 0, rows, False)
 
@@ -240,7 +241,6 @@
                 st[at] = small if first else st[at] + small
 
     add_state(0, rows, True)
-    pass_on(1)
     wait_block(y_own)
     send_block(y_own, core_peer, 22)
     load_w[0].wait()
@@ -250,11 +250,10 @@
         project(1, ks, rows + k * CHUNK, CHUNK, True)
         project(2, vs, rows + k * CHUNK, CHUNK, False)
         add_state(rows + k * CHUNK, CHUNK, False)
-        if k == 0:
-            pass_on(2)
     stb[...] = st[...].astype(BF16)
     c_core = remote(stb, cst, s_send.at[0], s_recv.at[0], core_peer)
     c_core.start()
+    pass_on(2)
     c_core.wait_recv()
 
     mine = pl.ds(pl.multiple_of(core * lanes, 128), lanes)
@@ -271,8 +270,8 @@
         def _():
             remote(zb, zst.at[k - 1], s_send.at[1 + k], s_recv.at[1 + k], z_peer(k)).start()
 
+    project(0, qs, 0, 2 * rows, True)
     pass_on(3)
-    project(0, qs, 0, 2 * rows, True)
 
     cum[...] = st[...] + cst[...].astype(F32) * core.astype(F32)
     prior = yst[...].astype(F32) * y.astype(F32)

time: 66.2 us -> 67.3 us (1.017)
  Pallas kernels: 64.1 us -> 65.1 us
    pallas_call x1, Pallas kernels: 64.1 us -> 65.1 us  [fused(): pl.pallas_call(kernel, out_shape=jax.ShapeDtypeStruct((rows, d), BF16), i...]
where the time goes in v4:
time: 67.3 us; the launch traced here: 67.1 us
  Pallas kernels  65.1 us (97%)
  local copies, waits for them, and re-layouts  2.03 us (3%)
    pallas_call x1, Pallas kernels, fused(): pl.pallas_call(kernel, out_shape=jax.ShapeDtypeStruct((rows, d), BF16), i...  65.1 us
    unnamed x1, local copies, waits for them, and re-layouts  2.03 us

profile of v4, /device:TPU:24, one launch (start us, length us, event | category | flops | bytes accessed | tf_op | source)
XLA Modules:
  0.0 67.1 jit_solution(17571444773174231276)
XLA Ops:
  0.0 65.1 %shard_map.37 = bf16[160,2240]{1,0:T(8,128)(2,1)} custom-call(bf16[160,2240]{1,0:T(8,128)(2,1)} %bitcast.4, bf16[3,448,4480]{2,1,0:T(8,128)(2,1)} %w_ref.1, bf16[140,896]{1,0:T(8,128)(2,1)} %bitcast.5), custom_call_target="tpu_custom_call" | custom-call | tf_op jit(solution)/shard_map/pallas_call | solution.py:380
  65.1 2.0 %copy.5 = bf16[1,2,80,2240]{3,2,1,0:T(8,128)(2,1)} copy(bf16[1,2,80,2240]{3,2,1,0:T(8,128)(2,1)} %bitcast.3) | data formatting | bytes 1433600
